TPU v7x, 32 devices: a whole 2x2x4 slice. The times are simulated.
32 devices in a mesh: groups: 2 (over x), gx: 16 (over z, y, core).
Axes of the slice: x: 2, y: 2, z: 4, core: 2. Of those that a mesh axis runs over, the one named last changes fastest.
Arguments:
- charges: bfloat16 [64, 16384], P(None, ('groups', 'gx')), parts along dimension 1
- cells: int32 [16384], P(('groups', 'gx')), parts along dimension 0, may hold values from 0 to 4095
- counts: int32 [1024], P(('groups', 'gx')), parts along dimension 0, may hold values from 8 to 16, as said below
- bricks: int32 [1024], P(('groups', 'gx')), parts along dimension 0, may hold values from 0 to 31, as said below
- spline: bfloat16 [3, 4, 16384], P(None, None, ('groups', 'gx')), parts along dimension 2, as said below
- spectral_filter: float32 [128, 128, 128], P(None, 'gx'), as said below
Outputs:
- potential: bfloat16 [64, 16384], P(None, ('groups', 'gx')), parts along dimension 1
- mesh_potential: bfloat16 [64, 256, 128, 128], P(None, ('groups', 'gx')), parts along dimension 1
- spline_grad: float32 [3, 4, 16384], P(None, None, ('groups', 'gx')), parts along dimension 2
There are 2 independent parts, one for each index of `groups`. A program takes and returns all parts, laid end to end along the dimension named above; an argument that names none is the same for every part. Nothing has to cross between parts.
Inputs may be any that keep to these rules, and one draw needn't show every extreme that they name: `counts`: every slab has a block whose slots are all live. Within each slab its 32 blocks name each of the slab's 32 bricks once. For each atom and dimension the four weights are the cubic B-spline weights of one fraction in [0, 1), for the mesh offsets -1, 0, 1, 2, rounded to bfloat16. `spectral_filter`: the filter has the same value at the wave numbers m and -m, indices taken modulo 128, 128, 128.
All inputs are finite; a program needn't handle non-finite values.
Results may differ from a plain program's by a relative error of at most 0.0052.
The roundings to bfloat16 on the way count: a program that leaves them out, or rounds other values in their place, can miss the bound.
Values may be sent and summed in bfloat16 or wider, within the bound.
A program may use at most 256 MiB of HBM per device.

v0:
```python
import math

import jax
import jax.numpy as jnp
from jax import lax
from jax.sharding import PartitionSpec as P

NX = 128
NY = 128
NZ = 128
BY = 4


PRECISE = lax.Precision.HIGH
SMEAR_WIDTH = 0.5


def shifted(block, axis, distance):
    devices = range(lax.axis_size(axis))
    route = [((i - distance) % len(devices), i) for i in devices]
    return lax.ppermute(block, axis, route)


def signed_wave(length):
    index = jnp.arange(length, dtype=jnp.int32)
    signed = jnp.where(index < length // 2, index, index - length)
    return 2.0 * math.pi / length * signed.astype(jnp.float32)


def coulomb_kernel(spectral_filter, row_offset):
    rows_y = spectral_filter.shape[1]
    wave_x = signed_wave(NX)[:, None, None]
    wave_y = lax.dynamic_slice_in_dim(signed_wave(NY), row_offset, rows_y)[None, :, None]
    wave_z = signed_wave(NZ)[None, None, :]
    squared = wave_x * wave_x + wave_y * wave_y + wave_z * wave_z
    safe_sq = jnp.where(squared > 0, squared, 1.0)
    value = (
        4.0
        * math.pi
        * spectral_filter
        * jnp.exp(-0.5 * SMEAR_WIDTH * SMEAR_WIDTH * squared)
        / safe_sq
    )
    return jnp.where(squared > 0, value, 0.0)


def complex_table(length, inverse):
    index = jnp.arange(length, dtype=jnp.int32)
    turn_count = index[:, None] * index[None, :] % length
    phase_angle = 2.0 * math.pi / length * turn_count.astype(jnp.float32)
    cosine = jnp.cos(phase_angle)
    sine_part = jnp.sin(phase_angle) * (1.0 if inverse else -1.0)
    table = jnp.stack(
        [jnp.stack([cosine, sine_part], axis=1), jnp.stack([-sine_part, cosine], axis=1)], axis=0
    )
    if inverse:
        table = table * (1.0 / length)
    return table


def transform(field, length, inverse, einsum_form):
    table = complex_table(length, inverse)
    return jnp.einsum(
        einsum_form,
        field.astype(jnp.float32),
        table,
        precision=PRECISE,
        preferred_element_type=jnp.float32,
    )


def atom_tables(charges, cells, counts, bricks, spline, shift_x, low_plane, planes):
    blocks = counts.shape[0]
    width = cells.shape[0] // blocks
    channels = charges.shape[0]
    slot_rank = jnp.arange(width, dtype=jnp.int32)
    live_mask = (slot_rank[None, :] < counts[:, None]).reshape(-1)
    weights = jnp.where(live_mask[None, None, :], spline.astype(jnp.float32), jnp.float32(0.0))
    kept_charges = jnp.where(live_mask[None, :], charges, jnp.zeros_like(charges))
    cell_x = cells // (BY * NZ)
    cell_y = cells // NZ % BY
    cell_z = cells % NZ
    offset = jnp.arange(4, dtype=jnp.int32)
    hit_x = (
        jnp.arange(planes, dtype=jnp.int32)[None, None, :]
        == (cell_x + shift_x - 1 - low_plane)[:, None, None] + offset[None, :, None]
    ).astype(jnp.float32)
    hit_y = (
        jnp.arange(BY + 3, dtype=jnp.int32)[None, None, :]
        == cell_y[:, None, None] + offset[None, :, None]
    ).astype(jnp.float32)
    hit_z = (
        jnp.arange(NZ, dtype=jnp.int32)[None, None, :]
        == (cell_z[:, None, None] + offset[None, :, None] - 1) % NZ
    ).astype(jnp.float32)
    weight_x = jnp.sum(weights[0].T[:, :, None] * hit_x, axis=1)
    weight_y = jnp.sum(weights[1].T[:, :, None] * hit_y, axis=1)
    weight_z = jnp.sum(weights[2].T[:, :, None] * hit_z, axis=1).astype(jnp.bfloat16)

    def blocked(source_table):
        return source_table.reshape((blocks, width) + source_table.shape[1:])

    charge_blocks = kept_charges.reshape(channels, blocks, width).transpose(1, 0, 2)
    row_start = bricks * BY
    return (
        charge_blocks,
        blocked(weight_x),
        blocked(weight_y),
        blocked(weight_z),
        blocked(hit_x),
        blocked(hit_y),
        blocked(hit_z),
        row_start,
    )


def spread_blocks(tables, grid_sum):
    charge_blocks, weight_x, weight_y, weight_z, hit_x, hit_y, hit_z, row_start = tables

    def add_block(grid_now, block_item):
        charge_block, wx_block, wy_block, wz_block, start_row = block_item
        lifted = (
            charge_block.astype(jnp.float32)[:, None, None, :]
            * wx_block.T[None, :, None, :]
            * wy_block.T[None, None, :, :]
        )
        lifted = lifted.astype(jnp.bfloat16)
        mesh_tile = jnp.einsum(
            "cxya,az->cxyz", lifted, wz_block, preferred_element_type=jnp.float32
        )
        before = lax.dynamic_slice_in_dim(grid_now, start_row, BY + 3, 2)
        return (lax.dynamic_update_slice_in_dim(grid_now, before + mesh_tile, start_row, 2), None)

    grid_sum, unused = lax.scan(
        add_block, grid_sum, (charge_blocks, weight_x, weight_y, weight_z, row_start)
    )
    return grid_sum


def fold_rows(padded):
    rows = padded.shape[2] - 3
    keep = ((0, 0), (0, 0))
    core_rows = padded[:, :, 1 : rows + 1]
    low_rows = jnp.pad(padded[:, :, 0:1], keep + ((rows - 1, 0), (0, 0)))
    high_rows = jnp.pad(padded[:, :, rows + 1 : rows + 3], keep + ((0, rows - 2), (0, 0)))
    return core_rows + low_rows + high_rows


def wrap_rows(field_now):
    rows = field_now.shape[2]
    return jnp.concatenate([field_now[:, :, rows - 1 :], field_now, field_now[:, :, :2]], axis=2)


def sample_blocks(tables, field_pad):
    charge_blocks, weight_x, weight_y, weight_z, hit_x, hit_y, hit_z, row_start = tables
    channels = charge_blocks.shape[1]

    def one_block(carry_value, block_item):
        charge_block, wx_block, wy_block, wz_block, hx_block, hy_block, hz_block, start_row = (
            block_item
        )
        mesh_tile = lax.dynamic_slice_in_dim(field_pad, start_row, BY + 3, 2)
        along_z = jnp.einsum(
            "cxyz,az->cxya", mesh_tile, wz_block, preferred_element_type=jnp.float32
        )
        block_potential = jnp.einsum(
            "cxya,ax,ay->ca", along_z, wx_block, wy_block, precision=PRECISE
        )
        charge_float = charge_block.astype(jnp.float32)
        charge_dot = jnp.einsum("cxya,ca->xya", along_z, charge_float, precision=PRECISE)
        grad_x = jnp.einsum("xya,ay,aix->ia", charge_dot, wy_block, hx_block, precision=PRECISE)
        grad_y = jnp.einsum("xya,ax,aiy->ia", charge_dot, wx_block, hy_block, precision=PRECISE)
        charge_tile = jnp.einsum(
            "ca,cxyz->axyz", charge_block, mesh_tile, preferred_element_type=jnp.float32
        )
        depth_sum = jnp.einsum("axyz,ax,ay->az", charge_tile, wx_block, wy_block, precision=PRECISE)
        grad_z = jnp.einsum("az,aiz->ia", depth_sum, hz_block, precision=PRECISE)
        return (carry_value, (block_potential, jnp.stack([grad_x, grad_y, grad_z])))

    unused, (block_potential, block_grad) = lax.scan(
        one_block,
        jnp.float32(0.0),
        (charge_blocks, weight_x, weight_y, weight_z, hit_x, hit_y, hit_z, row_start),
    )
    potential = block_potential.transpose(1, 0, 2).reshape(channels, -1)
    spline_grad = block_grad.transpose(1, 2, 0, 3).reshape(3, 4, -1)
    return (potential, spline_grad)


def mesh_transform(density, spectral_filter):
    channels, planes, rows, depth = density.shape
    pairs = density.reshape(channels // 2, 2, planes, rows, depth)
    field = transform(pairs, depth, False, "prxyz,rzsk->psxyk")
    field = transform(field, rows, False, "prxyz,rysk->psxkz")
    spectrum = field.astype(jnp.bfloat16)
    slab_rows = spectral_filter.shape[1]
    kernel = coulomb_kernel(spectral_filter, lax.axis_index("gx") * slab_rows)
    planes_all = spectral_filter.shape[0]
    spec_now = transform(
        lax.all_to_all(spectrum, "gx", split_axis=3, concat_axis=2, tiled=True),
        planes_all,
        False,
        "prxyz,rxsk->pskyz",
    )
    spec_now = transform(spec_now * kernel[None, None], planes_all, True, "prxyz,rxsk->pskyz")
    returned_block = spec_now.astype(jnp.bfloat16)
    returned = lax.all_to_all(returned_block, "gx", split_axis=2, concat_axis=3, tiled=True)
    field = transform(returned, rows, True, "prxyz,rysk->psxkz")
    field = transform(field, depth, True, "prxyz,rzsk->psxyk")
    return field.reshape(channels, planes, rows, depth).astype(jnp.bfloat16)


def body(charges, cells, counts, bricks, spline, spectral_filter):
    channels = charges.shape[0]
    planes = NX // lax.axis_size("gx")
    own_tables = atom_tables(charges, cells, counts, bricks, spline, 0, -1, planes + 3)
    padded = jnp.zeros((channels, planes + 3, NY + 3, NZ), jnp.float32)
    wide_density = fold_rows(spread_blocks(own_tables, padded))
    rim_below = shifted(wide_density[:, planes + 1 : planes + 3], "gx", 1)
    rim_above = shifted(wide_density[:, 0:1].astype(jnp.bfloat16), "gx", -1).astype(jnp.float32)
    keep = ((0, 0),)
    rest = ((0, 0), (0, 0))
    density = (
        wide_density[:, 1 : planes + 1]
        + jnp.pad(rim_below, keep + ((0, planes - 2),) + rest)
        + jnp.pad(rim_above, keep + ((planes - 1, 0),) + rest)
    )
    mesh_potential = mesh_transform(density, spectral_filter)
    below_plane = shifted(mesh_potential[:, planes - 1 : planes], "gx", 1)
    above_planes = shifted(mesh_potential[:, 0:2], "gx", -1)
    wide_field = jnp.concatenate([below_plane, mesh_potential, above_planes], axis=1)
    potential, spline_grad = sample_blocks(own_tables, wrap_rows(wide_field))
    return (potential.astype(jnp.bfloat16), mesh_potential, spline_grad)


def solution(mesh):
    return jax.shard_map(
        body,
        mesh=mesh,
        in_specs=(
            P(None, ("groups", "gx")),
            P(("groups", "gx")),
            P(("groups", "gx")),
            P(("groups", "gx")),
            P(None, None, ("groups", "gx")),
            P(None, "gx", None),
        ),
        out_specs=(
            P(None, ("groups", "gx")),
            P(None, ("groups", "gx"), None, None),
            P(None, None, ("groups", "gx")),
        ),
        check_vma=False,
    )
```

profile of v0, /device:TPU:30, one launch (start us, length us, event | category | flops | bytes accessed | tf_op | source)
XLA Modules:
  0.0 1958.0 jit_solution(6596293027027443555)
XLA Ops:
  5.8 15.5 broadcast_in_dim.45
  21.2 199.3 %while.22 = (s32[]{:T(128)}, f32[64,11,131,128]{3,0,2,1:T(8,128)}, s32[32]{0:T(128)S(1)}, bf16[32,64,16]{1,2,0:T(8,128)(2,1)S(1)}, f32[32,16,11]{1,0,2:T(8,128)S...) while((s32[]{:T(128)}, f32[64,11,131,128]{3,0,2,1:T(8,128)}, ...), condition=%wide.region_4.5_spmd, body=%wide.region_3.4_spmd.sunk | while | flops 20985860 | bytes 5204963 | solution.py:134
  67.1 3.8 add_dynamic-update-slice_fusion.2
  92.0 3.8 add_dynamic-update-slice_fusion.2
  135.6 3.9 add_dynamic-update-slice_fusion.2
  148.1 3.8 add_dynamic-update-slice_fusion.2
  160.6 3.8 add_dynamic-update-slice_fusion.2
  166.9 3.9 add_dynamic-update-slice_fusion.2
  179.3 3.8 add_dynamic-update-slice_fusion.2
  198.1 3.8 add_dynamic-update-slice_fusion.2
  225.8 33.8 %pad_add_fusion = f32[64,11,128,128]{3,0,2,1:T(8,128)} fusion(f32[64,11,2,128]{3,0,2,1:T(8,128)S(1)} %slice.45, f32[64,11,1,128]{3,0,2,1:T(8,128)S(1)} %slice.44, f32[64,11,131,128]{3,0,2,1:T(8,128)} %get-tuple-element.103), kind=kLoop, calls=%fused_computation.51 | loop fusion | flops 23068672 | bytes 93356032 | tf_op jit(solution)/shard_map/add | solution.py:146
  259.6 4.2 slice.57
  269.2 108.9 %collective-permute-done.1 = bf16[64,1,128,128]{3,0,2,1:T(8,128)(2,1)S(1)} collective-permute-done((bf16[64,1,128,128]{3,0,2,1:T(8,128)(2,1)S(1)}, bf16[64,1,128,128]{3,0,2,1:T(8,128)(2,1)S(1)}, u32[]{:S(2)}, u32[]{:S(2)}) %collective-permute-start.1) | collective-permute-done | bytes 2097184 | tf_op jit(solution)/shard_map/ppermute | solution.py:21
  379.2 24.5 %fusion.34 = f32[64,8,128,128]{3,0,2,1:T(8,128)} fusion(f32[64,11,128,128]{3,0,2,1:T(8,128)} %pad_add_fusion, f32[64,2,128,128]{3,0,2,1:T(8,128)S(1)} %collective-permute-done, bf16[64,1,128,128]{3,0,2,1:T(8,128)(2,1)S(1)} %collective-permute-done.1), kind=kLoop, calls=%fused_computation.53 | loop fusion | flops 25165824 | bytes 77594624 | tf_op jit(solution)/shard_map/add | solution.py:224
  403.7 34.9 %fusion.41 = f32[2,128,32,8,128,1]{4,1,5,0,3,2:T(8,128)} fusion(f32[32,2,8,128,128,1]{4,1,0,3,2,5:T(2,128)} %bitcast.303, f32[1,128,2,128]{1,3,0,2:T(8,128)S(1)} %get-tuple-element.254, f32[1,128,2,128]{1,3,0,2:T(8,128)S(1)} %get-tuple-element.255), kind=kOutput, calls=%fused_computation.64 | convolution fusion | flops 12884967424 | bytes 67371008 | tf_op jit(solution)/shard_map/prxyz,rzsk->psxyk/dot_general | solution.py:63
  438.6 22.2 %fusion.58 = bf16[32,2,8,128,128]{4,3,2,0,1:T(8,128)(2,1)} fusion(f32[2,128,32,8,128,1]{4,1,5,0,3,2:T(8,128)} %fusion.41, f32[1,128,2,128]{1,3,0,2:T(8,128)S(1)} %get-tuple-element.254, f32[1,128,2,128]{1,3,0,2:T(8,128)S(1)} %get-tuple-element.255), kind=kOutput, calls=%fused_computation.80 | convolution fusion | flops 12893356032 | bytes 50593792 | tf_op jit(solution)/shard_map/prxyz,rysk->psxkz/dot_general | solution.py:63
  460.8 17.2 copy.101
  478.0 6.0 all-to-all-start
  484.6 360.4 %all-to-all-done = bf16[32,2,8,128,128]{4,2,0,1,3:T(8,128)(2,1)} async-done(((bf16[32,2,8,128,128]{4,2,0,1,3:T(8,128)(2,1)}), bf16[32,2,8,128,128]{4,2,0,1,3:T(8,128)(2,1)}, u32[]{:S(2)}, u32[]{:S(2)}) %all-to-all-start) | async-done | bytes 16777248 | tf_op jit(solution)/shard_map/all_to_all | solution.py:200
  845.0 32.1 %copy.103 = bf16[32,2,16,8,8,128]{5,4,3,2,1,0:T(8,128)(2,1)} copy(bf16[32,2,16,8,8,128]{5,3,0,1,4,2:T(8,128)(2,1)} %bitcast.85) | data formatting | bytes 33554432 | tf_op jit(solution)/shard_map/all_to_all | solution.py:200
  877.2 18.7 fusion.53
  895.8 23.2 %fusion.49 = bf16[32,2,128,8,128]{4,2,3,0,1:T(8,128)(2,1)} fusion(f32[2,128,32,8,128,1]{4,1,5,0,3,2:T(8,128)} %fusion.53, f32[128,8,128]{2,0,1:T(8,128)S(1)} %copy.105, f32[1,128,2,128]{1,3,2,0:T(8,128)S(1)} %get-tuple-element.256, f32[1,128,2,128]{1,3,2,0:T(8,128)S(1)} %get-tuple-element.253), kind=kOutput, calls=%fused_computation.72 | convolution fusion | flops 12901810176 | bytes 51118080 | tf_op jit(solution)/shard_map/prxyz,rxsk->pskyz/dot_general | solution.py:63
  919.0 11.1 copy.107
  930.1 368.5 %all_to_all.36 = bf16[32,2,128,8,128]{4,3,0,1,2:T(8,128)(2,1)} all-to-all(bf16[32,2,128,8,128]{4,3,0,1,2:T(8,128)(2,1)S(1)} %copy.107), channel_id=1, replica_groups=mesh['groups'=2,'gx'=16] {'gx'}, dimensions={2} | all-to-all | bytes 33554432 | tf_op jit(solution)/shard_map/all_to_all | solution.py:207
  1298.6 20.4 %fusion.50 = f32[2,128,32,8,128,1]{4,1,0,5,3,2:T(8,128)} fusion(f32[1,128,2,128]{1,3,2,0:T(8,128)S(1)} %get-tuple-element.256, f32[1,128,2,128]{1,3,2,0:T(8,128)S(1)} %get-tuple-element.253, bf16[32,2,8,16,8,128]{5,4,0,1,2,3:T(8,128)(2,1)} %bitcast.309), kind=kOutput, calls=%fused_computation.73 | convolution fusion | flops 12885032960 | bytes 50593792 | tf_op jit(solution)/shard_map/prxyz,rysk->psxkz/dot_general | solution.py:63
  1319.0 21.9 %fusion.61 = bf16[32,2,8,128,128]{4,3,2,0,1:T(8,128)(2,1)} fusion(f32[2,128,32,8,128,1]{4,1,0,5,3,2:T(8,128)} %fusion.50, f32[1,128,2,128]{1,3,2,0:T(8,128)S(1)} %get-tuple-element.256, f32[1,128,2,128]{1,3,2,0:T(8,128)S(1)} %get-tuple-element.253), kind=kOutput, calls=%fused_computation.81 | convolution fusion | flops 12893421568 | bytes 50593792 | tf_op jit(solution)/shard_map/prxyz,rzsk->psxyk/dot_general | solution.py:63
  1340.9 8.1 copy.113
  1351.5 4.8 copy-done
  1361.4 63.8 %collective-permute-done.2 = bf16[64,1,128,128]{3,2,1,0:T(8,128)(2,1)S(1)} collective-permute-done((bf16[64,1,128,128]{3,2,1,0:T(8,128)(2,1)}, bf16[64,1,128,128]{3,2,1,0:T(8,128)(2,1)S(1)}, u32[]{:S(2)}, u32[]{:S(2)}) %collective-permute-start.2) | collective-permute-done | bytes 2097184 | tf_op jit(solution)/shard_map/ppermute | solution.py:21
  1425.2 22.5 %fusion.43 = bf16[64,11,131,128]{3,2,1,0:T(8,128)(2,1)} fusion(bf16[64,2,128,128]{3,2,1,0:T(8,128)(2,1)} %collective-permute-done.3, bf16[64,8,128,128]{3,2,1,0:T(8,128)(2,1)} %bitcast.307, bf16[64,1,128,128]{3,2,1,0:T(8,128)(2,1)S(1)} %collective-permute-done.2), kind=kLoop, calls=%fused_computation.67 | loop fusion | flops 212484096 | bytes 46678016 | tf_op jit(solution)/shard_map/concatenate | solution.py:151
  1447.7 22.5 %copy.116 = bf16[64,11,131,128]{3,0,2,1:T(8,128)(2,1)} copy(bf16[64,11,131,128]{3,2,1,0:T(8,128)(2,1)} %fusion.43) | data formatting | bytes 47218688 | tf_op jit(solution)/shard_map/while | solution.py:180
  1470.2 486.1 %while.23 = (s32[]{:T(128)}, bf16[32,64,16]{1,2,0:T(8,128)(2,1)S(1)}, f32[32,3,4,16]{3,2,1,0:T(4,128)S(1)}, f32[32,16,7]{1,2,0:T(8,128)}, f32[32,16,11]{1,0,2:T(...) while((s32[]{:T(128)}, ...), condition=%wide.region_6.7_spmd, body=%wide.region_5.6_spmd.sunk | while | flops 42330260 | bytes 4886563 | solution.py:180
  (1062 shorter events, 562.6 us)
Async XLA Ops:
  1.3 1.6 copy-start.8
  1.3 1.6 copy-start.10
  1.4 1.8 copy-start.6
  220.5 0.7 copy-start.2
  221.2 0.7 copy-start.3
  221.8 0.6 copy-start.4
  222.5 0.7 copy-start.5
  223.1 0.5 copy-start.12
  263.8 115.4 %collective-permute-start = (f32[64,2,128,128]{3,0,2,1:T(8,128)S(1)}, f32[64,2,128,128]{3,0,2,1:T(8,128)S(1)}, u32[]{:S(2)}, u32[]{:S(2)}) collective-permute-start(f32[64,2,128,128]{3,0,2,1:T(8,128)S(1)} %slice.57), channel_id=1, source_target_pairs={{15,0},{0,1},{1,2},{2,3},{3,4},{4,5},{5,6},{6,7},{7,8},{8,9},{9,10... | collective-permute-start | bytes 25165832 | tf_op jit(solution)/shard_map/ppermute | solution.py:21
  266.6 111.6 %collective-permute-start.1 = (bf16[64,1,128,128]{3,0,2,1:T(8,128)(2,1)S(1)}, bf16[64,1,128,128]{3,0,2,1:T(8,128)(2,1)S(1)}, u32[]{:S(2)}, u32[]{:S(2)}) collective-permute-start(bf16[64,1,128,128]{3,0,2,1:T(8,128)(2,1)S(1)} %slice.69), channel_id=1, source_target_pairs={{1,0},{2,1},{3,2},{4,3},{5,4},{6,5},{7,6},{8,7},{9,8},{10,9},{11,1... | collective-permute-start | bytes 6291464 | tf_op jit(solution)/shard_map/ppermute | solution.py:21
  460.8 23.4 %copy-start.1 = (f32[128,8,128]{2,1,0:T(8,128)S(1)}, f32[128,8,128]{2,1,0:T(8,128)}, u32[]{:S(2)}) copy-start(f32[128,8,128]{2,1,0:T(8,128)} %param.15) | copy-start | bytes 1572868
  478.0 367.0 %all-to-all-start = ((bf16[32,2,8,128,128]{4,2,0,1,3:T(8,128)(2,1)}), bf16[32,2,8,128,128]{4,2,0,1,3:T(8,128)(2,1)}, u32[]{:S(2)}, u32[]{:S(2)}) async-start(bf16[32,2,8,128,128]{4,2,0,1,3:T(8,128)(2,1)} %copy.101), calls=%async_computation | async-start | bytes 33554432 | tf_op jit(solution)/shard_map/all_to_all | solution.py:200
  1340.9 17.3 copy-start.11
  1340.9 17.4 copy-start.9
  1340.9 17.4 copy-start.7
  1348.9 7.4 copy-start
  1351.4 73.8 %collective-permute-start.3 = (bf16[64,2,128,128]{3,2,1,0:T(8,128)(2,1)}, bf16[64,2,128,128]{3,2,1,0:T(8,128)(2,1)}, u32[]{:S(2)}, u32[]{:S(2)}) collective-permute-start(bf16[64,2,128,128]{3,2,1,0:T(8,128)(2,1)} %slice.60), channel_id=1, source_target_pairs={{1,0},{2,1},{3,2},{4,3},{5,4},{6,5},{7,6},{8,7},{9,8},{10,9},{11,1... | collective-permute-start | bytes 12582920 | tf_op jit(solution)/shard_map/ppermute | solution.py:21
  1357.8 67.4 %collective-permute-start.2 = (bf16[64,1,128,128]{3,2,1,0:T(8,128)(2,1)}, bf16[64,1,128,128]{3,2,1,0:T(8,128)(2,1)S(1)}, u32[]{:S(2)}, u32[]{:S(2)}) collective-permute-start(bf16[64,1,128,128]{3,2,1,0:T(8,128)(2,1)} %slice.59), channel_id=1, source_target_pairs={{15,0},{0,1},{1,2},{2,3},{3,4},{4,5},{5,6},{6,7},{7,8},{8,9},{9,10... | collective-permute-start | bytes 6291464 | tf_op jit(solution)/shard_map/ppermute | solution.py:21
  1447.7 22.5 %copy-start.13 = (s32[32]{0:T(128)S(1)}, s32[32]{0:T(128)}, u32[]{:S(2)}) copy-start(s32[32]{0:T(128)} %copy-done.12) | copy-start | bytes 388
where the time goes:
time: 1980 us; the launch traced here: 1960 us
  waiting for transfers between devices  534 us (27%)
  matrix products  523 us (26%)
  blocking collectives  368 us (19%)
  local copies, waits for them, and re-layouts  261 us (13%)
  other arithmetic  144 us (7%)
  loops' own time  118 us (6%)
    all_to_all x1, blocking collectives, mesh_transform(): lax.all_to_all(returned_block, 'gx', split_axis=2, concat_axis=3, tiled=T...  368 us
    all_to_all x1, waiting for transfers between devices, mesh_transform(): lax.all_to_all(spectrum, 'gx', split_axis=3, concat_axis=2, tiled=True)  360 us
    ppermute x4, waiting for transfers between devices, shifted(): return lax.ppermute(block, axis, route)  174 us
    dot_general x6, matrix products, transform(): jnp.einsum(einsum_form, field.astype(jnp.float32), table, precision=PRECI...  141 us
    dot_general x32, matrix products, add_block(): jnp.einsum('cxya,az->cxyz', lifted, wz_block, preferred_element_type=jnp....  122 us
    dot_general x32, matrix products, one_block(): jnp.einsum('cxyz,az->cxya', mesh_tile, wz_block, preferred_element_type=j...  76.7 us
    dynamic_slice x192, local copies, waits for them, and re-layouts, spread_blocks(): lax.scan(add_block, grid_sum, (charge_blocks, weight_x, weight_y, weight_...  66 us
    dot_general x32, matrix products, one_block(): jnp.einsum('cxya,ca->xya', along_z, charge_float, precision=PRECISE)  64.4 us
  transfers between devices with their start and end apart: 5, of which 4 were waited for; matrix products, arithmetic and copies ran while one was open for 0% of the time, Pallas kernels for 0%

commit v1 on v0

v1 whole, which is shorter than its diff:
```python
import math

import jax
import jax.numpy as jnp
from jax import lax
from jax.experimental import pallas as pl
from jax.experimental.pallas import tpu as pltpu
from jax.sharding import PartitionSpec as P

NX = 128
NY = 128
NZ = 128
BY = 4
PARTS = 2


PRECISE = lax.Precision.HIGH
SMEAR_WIDTH = 0.5


def shifted(block, axis, distance):
    devices = range(lax.axis_size(axis))
    route = [((i - distance) % len(devices), i) for i in devices]
    return lax.ppermute(block, axis, route)


def signed_wave(length):
    index = jnp.arange(length, dtype=jnp.int32)
    signed = jnp.where(index < length // 2, index, index - length)
    return 2.0 * math.pi / length * signed.astype(jnp.float32)


def coulomb_kernel(spectral_filter, row_offset):
    rows_y = spectral_filter.shape[1]
    wave_x = signed_wave(NX)[:, None, None]
    wave_y = lax.dynamic_slice_in_dim(signed_wave(NY), row_offset, rows_y)[None, :, None]
    wave_z = signed_wave(NZ)[None, None, :]
    squared = wave_x * wave_x + wave_y * wave_y + wave_z * wave_z
    safe_sq = jnp.where(squared > 0, squared, 1.0)
    value = (
        4.0
        * math.pi
        * spectral_filter
        * jnp.exp(-0.5 * SMEAR_WIDTH * SMEAR_WIDTH * squared)
        / safe_sq
    )
    return jnp.where(squared > 0, value, 0.0)


def complex_table(length, inverse):
    index = jnp.arange(length, dtype=jnp.int32)
    turn_count = index[:, None] * index[None, :] % length
    phase_angle = 2.0 * math.pi / length * turn_count.astype(jnp.float32)
    cosine = jnp.cos(phase_angle)
    sine_part = jnp.sin(phase_angle) * (1.0 if inverse else -1.0)
    table = jnp.stack(
        [jnp.stack([cosine, sine_part], axis=1), jnp.stack([-sine_part, cosine], axis=1)], axis=0
    )
    if inverse:
        table = table * (1.0 / length)
    return table


def transform(field, length, inverse, einsum_form):
    table = complex_table(length, inverse)
    return jnp.einsum(
        einsum_form,
        field.astype(jnp.float32),
        table,
        precision=PRECISE,
        preferred_element_type=jnp.float32,
    )


def packed_atoms(charges, cells, counts, spline):
    blocks = counts.shape[0]
    width = cells.shape[0] // blocks
    rank = jnp.arange(width, dtype=jnp.int32)
    live = (rank[None, :] < counts[:, None]).reshape(1, -1)
    kept_charges = jnp.where(live, charges, jnp.zeros_like(charges))
    kept_weights = jnp.where(live, spline.reshape(12, -1), jnp.zeros((), spline.dtype))
    place = jnp.stack([cells // (BY * NZ), cells // NZ % BY, cells % NZ]).astype(jnp.bfloat16)
    packed = jnp.concatenate([place, kept_weights, kept_charges], axis=0)
    return packed.reshape(packed.shape[0], blocks, width)


def by_brick(packed, bricks):
    blocks = bricks.shape[0]
    chosen = (bricks[:, None] == jnp.arange(blocks, dtype=jnp.int32)[None, :]).astype(jnp.bfloat16)
    return jnp.einsum(
        "fba,bn->fna", packed, chosen, preferred_element_type=jnp.float32
    ).astype(jnp.bfloat16)


def unpack(packed):
    place = packed[:3].astype(jnp.int32)
    weights = packed[3:15].astype(jnp.float32).reshape((3, 4) + packed.shape[1:])
    return place, weights, packed[15:]


def dense_weights(weights, start, size):
    row = jnp.arange(size, dtype=jnp.int32)[None, :, None]
    total = 0.0
    for offset in range(4):
        hit = row == start[:, None, :] + offset
        total = total + jnp.where(hit, weights[offset][:, None, :], 0.0)
    return total


def spread_tables(packed, shift_x, planes):
    place, weights, charge = unpack(packed)
    charge = charge.transpose(1, 0, 2)
    weight_x = dense_weights(weights[0], place[0] + (shift_x - 1), planes)
    weight_y = dense_weights(weights[1], place[1], BY + 3)
    column = jnp.arange(NZ, dtype=jnp.int32)[None, None, :]
    weight_z = 0.0
    for offset in range(4):
        hit = column == (place[2][:, :, None] + (offset - 1)) % NZ
        weight_z = weight_z + jnp.where(hit, weights[2, offset][:, :, None], 0.0)
    weight_z = weight_z.astype(jnp.bfloat16)

    def around(table, axis):
        return jnp.concatenate(
            [jnp.roll(table, 1, 0), table, jnp.roll(table, -1, 0)], axis=axis
        )

    none = jnp.zeros_like(weight_y)
    previous = jnp.roll(jnp.concatenate([weight_y[:, 5:7], none[:, :2]], axis=1), 1, 0)
    following = jnp.roll(jnp.concatenate([none[:, :3], weight_y[:, :1]], axis=1), -1, 0)
    rows = jnp.concatenate([previous, weight_y[:, 1:5], following], axis=2)
    pair = around(weight_x, 2)[:, :, None, :] * rows[:, None, :, :]
    pair = pair.reshape(pair.shape[0], planes * BY, pair.shape[3])
    return around(charge, 2), pair, around(weight_z, 1)


def spread_kernel(*refs):
    out_refs = refs[9:]
    planes, unused, share = out_refs[0].shape[:3]

    def part(group, first, count):
        charge = refs[3 * group][0].astype(jnp.float32)
        pair = refs[3 * group + 1][0, BY * first : BY * (first + count)]
        lifted = (charge[None] * pair[:, None, :]).astype(jnp.bfloat16)
        lifted = lifted.reshape(-1, lifted.shape[2])
        tile = jnp.dot(lifted, refs[3 * group + 2][0], preferred_element_type=jnp.float32)
        return tile.reshape((count, BY) + (charge.shape[0], NZ))

    for plane in range(planes):
        tile = part(0, plane, 1)
        if plane < 2:
            tile = tile + part(1, plane, 1)
        if plane == planes - 1:
            tile = tile + part(2, 0, 1)
        for index, out_ref in enumerate(out_refs):
            out_ref[plane : plane + 1] = tile[:, :, share * index : share * (index + 1)]


def spread(packed, bricks, planes):
    ordered = by_brick(packed, bricks)
    below = shifted(ordered, "gx", 1)
    above = shifted(ordered, "gx", -1)
    tables = [
        *spread_tables(ordered, 0, planes),
        *spread_tables(below, -planes, 2),
        *spread_tables(above, 1, 1),
    ]
    blocks = bricks.shape[0]
    share = tables[0].shape[1] // PARTS
    return pl.pallas_call(
        spread_kernel,
        grid=(blocks,),
        in_specs=[pl.BlockSpec((1,) + t.shape[1:], lambda n: (n, 0, 0)) for t in tables],
        out_specs=[pl.BlockSpec((planes, BY, share, NZ), lambda n: (0, n, 0, 0))] * PARTS,
        out_shape=[jax.ShapeDtypeStruct((planes, NY, share, NZ), jnp.float32)] * PARTS,
        compiler_params=pltpu.CompilerParams(vmem_limit_bytes=32 * 1024 * 1024),
    )(*tables)


def sample_kernel(bricks_ref, *refs):
    fields = refs[:9]
    charge_ref, column_ref, wx_ref, wy_ref, pot_ref, gx_ref, gy_ref, gz_ref = refs[9:]
    charge = charge_ref[0].astype(jnp.float32)
    wx = wx_ref[0]
    wy = wy_ref[0]
    lanes = charge.shape[1]
    hit = lax.broadcasted_iota(jnp.int32, (NZ, lanes), 0) == column_ref[0]
    hit = jnp.where(hit, 1.0, 0.0).astype(jnp.bfloat16)
    potential = jnp.zeros(charge.shape, jnp.float32)
    along_y = jnp.zeros(wy.shape, jnp.float32)
    along_z = jnp.zeros((1, lanes), jnp.float32)
    top = 0
    for group in range(3):
        before, here, after = fields[3 * group : 3 * group + 3]
        for plane in range(here.shape[0]):
            tile = jnp.concatenate(
                [before[plane, BY - 1 : BY], here[plane], after[plane, 0:2]], axis=0
            )
            rows, channels = tile.shape[:2]
            taken = jnp.dot(
                tile.reshape(rows * channels, NZ), hit, preferred_element_type=jnp.float32
            ).reshape(rows, channels, lanes)
            wx_here = wx[top : top + 1]
            weight = wx_here * wy
            potential = potential + jnp.sum(taken * weight[:, None, :], axis=0)
            dots = jnp.sum(taken * charge[None], axis=1)
            over_y = jnp.sum(dots * wy, axis=0, keepdims=True)
            gx_ref[0, top : top + 1] = over_y
            along_y = along_y + wx_here * dots
            along_z = along_z + wx_here * over_y
            top += 1
    pot_ref[0] = potential
    gy_ref[0] = along_y
    gz_ref[0] = along_z


def sample(packed, bricks, fields):
    place, weights, charge = unpack(packed)
    blocks, width = bricks.shape[0], packed.shape[2]
    channels = charge.shape[0]
    planes = sum(field.shape[0] for field in fields)
    charge_lanes = jnp.tile(charge.transpose(1, 0, 2), (1, 1, 4))
    offset = jnp.arange(4, dtype=jnp.int32)
    column = (place[2][:, None, :] + offset[None, :, None] - 1) % NZ
    column = column.reshape(blocks, 1, 4 * width)
    weight_z = weights[2].transpose(1, 0, 2)
    weight_x = jnp.tile(dense_weights(weights[0], place[0], planes), (1, 1, 4))
    weight_y = jnp.tile(dense_weights(weights[1], place[1], BY + 3), (1, 1, 4))
    lanes = 4 * width
    bricks_all = NY // BY

    def field_spec(field, step):
        return pl.BlockSpec(
            (field.shape[0], BY, channels, NZ),
            lambda n, b: (0, lax.rem(b[n] + (step + bricks_all), bricks_all), 0, 0),
        )

    def table_spec(rows):
        return pl.BlockSpec((1, rows, lanes), lambda n, b: (n, 0, 0))

    sizes = [channels, planes, BY + 3, 1]
    pot, gx, gy, gz = pl.pallas_call(
        sample_kernel,
        grid_spec=pltpu.PrefetchScalarGridSpec(
            num_scalar_prefetch=1,
            grid=(blocks,),
            in_specs=[field_spec(f, step) for f in fields for step in (-1, 0, 1)]
            + [table_spec(r) for r in (channels, 1, planes, BY + 3)],
            out_specs=[table_spec(r) for r in sizes],
        ),
        out_shape=[jax.ShapeDtypeStruct((blocks, r, lanes), jnp.float32) for r in sizes],
        compiler_params=pltpu.CompilerParams(vmem_limit_bytes=32 * 1024 * 1024),
    )(bricks, *[f for f in fields for _ in range(3)], charge_lanes, column, weight_x, weight_y)

    def split(table):
        return table.reshape(blocks, table.shape[1], 4, width)

    weight_k = weight_z[:, None]
    potential = jnp.sum(split(pot) * weight_k, axis=2)
    potential = potential.transpose(1, 0, 2).reshape(channels, -1)
    over_x = jnp.sum(split(gx) * weight_k, axis=2)
    over_y = jnp.sum(split(gy) * weight_k, axis=2)

    def pick(table, start):
        row = jnp.arange(table.shape[1], dtype=jnp.int32)[None, :, None]
        picked = [
            jnp.sum(jnp.where(row == start[:, None, :] + i, table, 0.0), axis=1) for i in range(4)
        ]
        return jnp.stack(picked)

    grad_x = pick(over_x, place[0])
    grad_y = pick(over_y, place[1])
    grad_z = split(gz)[:, 0].transpose(1, 0, 2)
    spline_grad = jnp.stack([grad_x, grad_y, grad_z]).reshape(3, 4, -1)
    return potential, spline_grad


def mesh_transform(density, spectral_filter):
    planes, rows, share, depth = density[0].shape
    devices = lax.axis_size("gx")
    planes_all, slab_rows = spectral_filter.shape[:2]
    kernel = coulomb_kernel(spectral_filter, lax.axis_index("gx") * slab_rows)
    part = share // 2
    spectra = []
    for piece in density:
        pairs = piece.reshape(planes, rows, part, 2, depth)
        field = transform(pairs, depth, False, "xyprz,rzsk->psxyk")
        field = transform(field, rows, False, "prxyz,rysk->psxkz").astype(jnp.bfloat16)
        field = field.reshape(part, 2, planes, devices, slab_rows, depth)
        spectra.append(field.transpose(3, 0, 1, 2, 4, 5))
    spectra = [lax.all_to_all(s, "gx", split_axis=0, concat_axis=0, tiled=True) for s in spectra]
    returned = []
    for spectrum in spectra:
        field = spectrum.transpose(1, 2, 0, 3, 4, 5)
        field = field.reshape(part, 2, planes_all, slab_rows, depth)
        field = transform(field, planes_all, False, "prxyz,rxsk->pskyz")
        field = transform(field * kernel[None, None], planes_all, True, "prxyz,rxsk->pskyz")
        field = field.astype(jnp.bfloat16).reshape(part, 2, devices, planes, slab_rows, depth)
        returned.append(field.transpose(2, 0, 1, 3, 4, 5))
    returned = [lax.all_to_all(s, "gx", split_axis=0, concat_axis=0, tiled=True) for s in returned]
    potentials = []
    for spectrum in returned:
        field = spectrum.transpose(1, 2, 3, 0, 4, 5).reshape(part, 2, planes, rows, depth)
        field = transform(field, rows, True, "prxyz,rysk->psxkz")
        field = transform(field, depth, True, "prxyz,rzsk->psxyk")
        potentials.append(field.reshape(2 * part, planes, rows, depth).astype(jnp.bfloat16))
    return jnp.concatenate(potentials, axis=0)


def body(charges, cells, counts, bricks, spline, spectral_filter):
    planes = NX // lax.axis_size("gx")
    packed = packed_atoms(charges, cells, counts, spline)
    density = spread(packed, bricks, planes)
    mesh_potential = mesh_transform(density, spectral_filter)
    top_plane = mesh_potential[:, planes - 1 : planes].transpose(1, 2, 0, 3)
    low_planes = mesh_potential[:, 0:2].transpose(1, 2, 0, 3)
    below_plane = shifted(top_plane, "gx", 1)
    above_planes = shifted(low_planes, "gx", -1)
    fields = [below_plane, mesh_potential.transpose(1, 2, 0, 3), above_planes]
    potential, spline_grad = sample(packed, bricks, fields)
    return (potential.astype(jnp.bfloat16), mesh_potential, spline_grad)


def solution(mesh):
    return jax.shard_map(
        body,
        mesh=mesh,
        in_specs=(
            P(None, ("groups", "gx")),
            P(("groups", "gx")),
            P(("groups", "gx")),
            P(("groups", "gx")),
            P(None, None, ("groups", "gx")),
            P(None, "gx", None),
        ),
        out_specs=(
            P(None, ("groups", "gx")),
            P(None, ("groups", "gx"), None, None),
            P(None, None, ("groups", "gx")),
        ),
        check_vma=False,
    )
```

time: 1980 us -> 1040 us (0.53)
  blocking collectives: 368 us -> 0 us
  matrix products: 523 us -> 167 us
  loops' own time: 118 us -> 0 us
  other arithmetic: 144 us -> 40.4 us
  local copies, waits for them, and re-layouts: 261 us -> 187 us
  Pallas kernels: 0 us -> 58.3 us
  starting transfers between devices: 8.28 us -> 30.1 us
    dot_general x288 -> x1, matrix products: 381 us -> 0.82 us  [by_brick(): jnp.einsum('fba,bn->fna', packed, chosen, preferred_element_type=jnp.floa...]
    all_to_all x1 -> x0, blocking collectives: 368 us -> none  [mesh_transform(): lax.all_to_all(returned_block, 'gx', split_axis=2, concat_axis=3, tiled=T...]
    all_to_all x1 -> x4, waiting for transfers between devices: 360 us -> 534 us  [mesh_transform(): lax.all_to_all(s, 'gx', split_axis=0, concat_axis=0, tiled=True)]
    ppermute x4, waiting for transfers between devices: 174 us -> 14.2 us  [shifted(): return lax.ppermute(block, axis, route)]
    another operation x2 -> x0, loops' own time: 118 us -> none  [the longest x1 63.4 us: sample_blocks(): lax.scan(one_block, jnp.float32(0.0), (charge_blocks, weight_x, weight_y,...]
    dynamic_slice x192 -> x0, local copies, waits for them, and re-layouts: 66 us -> none  [spread_blocks(): lax.scan(add_block, grid_sum, (charge_blocks, weight_x, weight_y, weight_...]
    pallas_call x0 -> x2, Pallas kernels: none -> 58.3 us  [the longest x1 39.6 us: sample(): pl.pallas_call(sample_kernel, grid_spec=pltpu.PrefetchScalarGridSpec(num_...]
    add x5 -> x12, other arithmetic: 58.3 us -> 0.52 us  [the longest x8 0.49 us: dense_weights(): total = total + jnp.where(hit, weights[offset][:, None, :], 0.0)]
  transfers between devices with their start and end apart: 5 -> 8, of which waited for: 4 -> 5; matrix products, arithmetic and copies ran while one was open for 0% -> 25% of each run, Pallas kernels for 0% -> 0%
where the time goes in v1:
time: 1040 us; the launch traced here: 1030 us
  waiting for transfers between devices  548 us (53%)
  local copies, waits for them, and re-layouts  187 us (18%)
  matrix products  167 us (16%)
  Pallas kernels  58.3 us (6%)
  other arithmetic  40.4 us (4%)
  starting transfers between devices  30.1 us (3%)
    all_to_all x4, waiting for transfers between devices, mesh_transform(): lax.all_to_all(s, 'gx', split_axis=0, concat_axis=0, tiled=True)  534 us
    dot_general x12, matrix products, transform(): jnp.einsum(einsum_form, field.astype(jnp.float32), table, precision=PRECI...  166 us
    unnamed x53, local copies, waits for them, and re-layouts  47.3 us
    convert_element_type x2, local copies, waits for them, and re-layouts, mesh_transform(): field.reshape(2 * part, planes, rows, depth).astype(jnp.bfloat16)  42.3 us
    pallas_call x1, Pallas kernels, sample(): pl.pallas_call(sample_kernel, grid_spec=pltpu.PrefetchScalarGridSpec(num_...  39.6 us
    reshape x2, local copies, waits for them, and re-layouts, mesh_transform(): field.astype(jnp.bfloat16)  32.8 us
    all_to_all x4, starting transfers between devices, mesh_transform(): lax.all_to_all(s, 'gx', split_axis=0, concat_axis=0, tiled=True)  29 us
  transfers between devices with their start and end apart: 8, of which 5 were waited for; matrix products, arithmetic and copies ran while one was open for 25% of the time, Pallas kernels for 0%

profile of v1, /device:TPU:30, one launch (start us, length us, event | category | flops | bytes accessed | tf_op | source)
XLA Modules:
  0.0 1032.9 jit_solution(15684852967980803950)
XLA Ops:
  40.7 18.7 %shard_map.85 = (f32[8,128,32,128]{3,2,1,0:T(8,128)S(1)}, f32[8,128,32,128]{3,2,1,0:T(8,128)}) custom-call(bf16[32,64,48]{2,1,0:T(8,128)(2,1)S(1)} %get-tuple-element.181.refs_0_, f32[32,32,48]{2,1,0:T(8,128)S(1)} %bitcast.416, bf16[32,48,128]{2,1,0:T(8,128)(2,1)S(1)} %get-tuple-element.183.refs_2_, bf16[32,64,48]{2,1,0:T(8,128)(2,1)S(1)} %get-tuple-element.182.refs_3_, ...), custom_call_target="tpu_custom_call" | custom-call | tf_op jit(solution)/shard_map/pallas_call | solution.py:169
  65.2 21.1 %fusion.14 = f32[2,128,8,128,16,1]{3,1,5,0,2,4:T(8,128)} fusion(f32[8,128,16,2,128,1]{4,3,2,1,0,5:T(2,128)} %bitcast.415, f32[1,128,2,128]{1,3,0,2:T(8,128)S(1)} %get-tuple-element.116, f32[1,128,2,128]{1,3,0,2:T(8,128)S(1)} %get-tuple-element.117), kind=kOutput, calls=%fused_computation.27 | convolution fusion | flops 6442516480 | bytes 33816576 | tf_op jit(solution)/shard_map/xyprz,rzsk->psxyk/dot_general | solution.py:66
  86.3 13.2 %fusion.16 = bf16[16,2,8,16,8,128]{5,4,3,2,0,1:T(8,128)(2,1)} fusion(f32[2,128,8,128,16,1]{3,1,5,0,2,4:T(8,128)} %fusion.14, f32[1,128,2,128]{1,3,0,2:T(8,128)S(1)} %get-tuple-element.116, f32[1,128,2,128]{1,3,0,2:T(8,128)S(1)} %get-tuple-element.117), kind=kOutput, calls=%fused_computation.29 | convolution fusion | flops 6446710784 | bytes 25427968 | tf_op jit(solution)/shard_map/prxyz,rysk->psxkz/dot_general | solution.py:66
  99.5 9.1 copy.678
  108.6 9.9 all-to-all-start
  118.5 21.0 %fusion.12 = f32[2,128,8,128,16,1]{3,1,5,0,2,4:T(8,128)} fusion(f32[8,128,16,2,128,1]{4,3,2,1,0,5:T(2,128)} %bitcast.430, f32[1,128,2,128]{1,3,0,2:T(8,128)S(1)} %get-tuple-element.116, f32[1,128,2,128]{1,3,0,2:T(8,128)S(1)} %get-tuple-element.117), kind=kOutput, calls=%fused_computation.21 | convolution fusion | flops 6442516480 | bytes 33816576 | tf_op jit(solution)/shard_map/xyprz,rzsk->psxyk/dot_general | solution.py:66
  139.5 13.3 %fusion.19 = bf16[16,2,8,16,8,128]{5,4,3,2,0,1:T(8,128)(2,1)} fusion(f32[2,128,8,128,16,1]{3,1,5,0,2,4:T(8,128)} %fusion.12, f32[1,128,2,128]{1,3,0,2:T(8,128)S(1)} %get-tuple-element.116, f32[1,128,2,128]{1,3,0,2:T(8,128)S(1)} %get-tuple-element.117), kind=kOutput, calls=%fused_computation.32 | convolution fusion | flops 6446710784 | bytes 25427968 | tf_op jit(solution)/shard_map/prxyz,rysk->psxkz/dot_general | solution.py:66
  152.8 9.1 copy.676
  161.9 137.7 %all-to-all-done = bf16[16,16,2,8,8,128]{5,4,3,2,1,0:T(8,128)(2,1)} async-done(((bf16[16,16,2,8,8,128]{5,4,3,2,1,0:T(8,128)(2,1)}), bf16[16,16,2,8,8,128]{5,4,3,2,1,0:T(8,128)(2,1)}, u32[]{:S(2)}, u32[]{:S(2)}) %all-to-all-start) | async-done | bytes 8388640 | tf_op jit(solution)/shard_map/all_to_all | solution.py:290
  306.3 9.7 copy.518
  316.0 10.7 %fusion.30 = f32[2,128,16,8,128,1]{4,1,5,0,3,2:T(8,128)} fusion(bf16[16,2,128,8,128,1]{4,3,2,1,0,5:T(8,128)(2,1)} %bitcast.425, f32[1,128,2,128]{1,3,0,2:T(8,128)S(1)} %get-tuple-element.116, f32[1,128,2,128]{1,3,0,2:T(8,128)S(1)} %get-tuple-element.117), kind=kOutput, calls=%fused_computation.43 | convolution fusion | flops 6442516480 | bytes 25427968 | tf_op jit(solution)/shard_map/prxyz,rxsk->pskyz/dot_general | solution.py:66
  326.7 14.1 %fusion.17 = bf16[16,2,16,8,8,128]{5,3,2,4,0,1:T(8,128)(2,1)} fusion(f32[2,128,16,8,128,1]{4,1,5,0,3,2:T(8,128)} %fusion.30, f32[128,8,128]{2,0,1:T(8,128)S(1)} %copy.520, f32[1,128,2,128]{1,3,2,0:T(8,128)S(1)} %get-tuple-element.118, f32[1,128,2,128]{1,3,2,0:T(8,128)S(1)} %get-tuple-element.115), kind=kOutput, calls=%fused_computation.30 | convolution fusion | flops 6450970624 | bytes 25952256 | tf_op jit(solution)/shard_map/prxyz,rxsk->pskyz/dot_general | solution.py:66
  340.8 16.4 %copy.677 = bf16[16,2,16,8,8,128]{5,4,3,1,0,2:T(8,128)(2,1)} copy(bf16[16,2,16,8,8,128]{5,3,2,4,0,1:T(8,128)(2,1)} %fusion.17) | data formatting | bytes 16777216 | tf_op jit(solution)/shard_map/reshape | solution.py:297
  357.2 129.8 %all-to-all-done.2 = bf16[16,16,2,8,8,128]{5,4,3,2,1,0:T(8,128)(2,1)} async-done(((bf16[16,16,2,8,8,128]{5,4,3,2,1,0:T(8,128)(2,1)}), bf16[16,16,2,8,8,128]{5,4,3,2,1,0:T(8,128)(2,1)}, u32[]{:S(2)}, u32[]{:S(2)}) %all-to-all-start.2) | async-done | bytes 8388640 | tf_op jit(solution)/shard_map/all_to_all | solution.py:290
  487.0 6.6 all-to-all-start.1
  493.6 9.7 copy.531
  503.2 10.7 %fusion.27 = f32[2,128,16,8,128,1]{4,1,5,0,3,2:T(8,128)} fusion(bf16[16,2,128,8,128,1]{4,3,2,1,0,5:T(8,128)(2,1)} %bitcast.424, f32[1,128,2,128]{1,3,0,2:T(8,128)S(1)} %get-tuple-element.116, f32[1,128,2,128]{1,3,0,2:T(8,128)S(1)} %get-tuple-element.117), kind=kOutput, calls=%fused_computation.40 | convolution fusion | flops 6442516480 | bytes 25427968 | tf_op jit(solution)/shard_map/prxyz,rxsk->pskyz/dot_general | solution.py:66
  514.0 14.1 %fusion.20 = bf16[16,2,16,8,8,128]{5,3,2,4,0,1:T(8,128)(2,1)} fusion(f32[2,128,16,8,128,1]{4,1,5,0,3,2:T(8,128)} %fusion.27, f32[128,8,128]{2,0,1:T(8,128)S(1)} %copy.520, f32[1,128,2,128]{1,3,2,0:T(8,128)S(1)} %get-tuple-element.118, f32[1,128,2,128]{1,3,2,0:T(8,128)S(1)} %get-tuple-element.115), kind=kOutput, calls=%fused_computation.33 | convolution fusion | flops 6450970624 | bytes 25952256 | tf_op jit(solution)/shard_map/prxyz,rxsk->pskyz/dot_general | solution.py:66
  528.1 16.4 %copy.675 = bf16[16,2,16,8,8,128]{5,4,3,1,0,2:T(8,128)(2,1)} copy(bf16[16,2,16,8,8,128]{5,3,2,4,0,1:T(8,128)(2,1)} %fusion.20) | data formatting | bytes 16777216 | tf_op jit(solution)/shard_map/reshape | solution.py:297
  544.5 130.2 %all-to-all-done.1 = bf16[16,16,2,8,8,128]{5,4,3,2,1,0:T(8,128)(2,1)} async-done(((bf16[16,16,2,8,8,128]{5,4,3,2,1,0:T(8,128)(2,1)}), bf16[16,16,2,8,8,128]{5,4,3,2,1,0:T(8,128)(2,1)}, u32[]{:S(2)}, u32[]{:S(2)}) %all-to-all-start.1) | async-done | bytes 8388640 | tf_op jit(solution)/shard_map/all_to_all | solution.py:299
  674.6 6.4 all-to-all-start.3
  681.0 10.7 %fusion.24 = f32[2,128,16,8,128,1]{4,1,0,5,3,2:T(8,128)} fusion(f32[1,128,2,128]{1,3,2,0:T(8,128)S(1)} %get-tuple-element.118, f32[1,128,2,128]{1,3,2,0:T(8,128)S(1)} %get-tuple-element.115, bf16[16,16,2,8,8,128]{5,4,3,2,1,0:T(8,128)(2,1)} %all-to-all-done.1), kind=kOutput, calls=%fused_computation.37 | convolution fusion | flops 6442582016 | bytes 25427968 | tf_op jit(solution)/shard_map/prxyz,rysk->psxkz/dot_general | solution.py:66
  691.8 13.2 %fusion.18 = bf16[16,2,8,128,128]{3,4,2,0,1:T(8,128)(2,1)} fusion(f32[2,128,16,8,128,1]{4,1,0,5,3,2:T(8,128)} %fusion.24, f32[1,128,2,128]{1,3,2,0:T(8,128)S(1)} %get-tuple-element.118, f32[1,128,2,128]{1,3,2,0:T(8,128)S(1)} %get-tuple-element.115), kind=kOutput, calls=%fused_computation.31 | convolution fusion | flops 6446776320 | bytes 25427968 | tf_op jit(solution)/shard_map/prxyz,rzsk->psxyk/dot_general | solution.py:66
  705.0 21.2 %copy.527 = bf16[16,2,8,128,128]{4,1,0,3,2:T(2,128)(2,1)} copy(bf16[16,2,8,128,128]{3,4,2,0,1:T(8,128)(2,1)} %fusion.18) | data formatting | bytes 16777216 | tf_op jit(solution)/shard_map/convert_element_type | solution.py:305
  726.2 135.9 %all-to-all-done.3 = bf16[16,16,2,8,8,128]{5,4,3,2,1,0:T(8,128)(2,1)} async-done(((bf16[16,16,2,8,8,128]{5,4,3,2,1,0:T(8,128)(2,1)}), bf16[16,16,2,8,8,128]{5,4,3,2,1,0:T(8,128)(2,1)}, u32[]{:S(2)}, u32[]{:S(2)}) %all-to-all-start.3) | async-done | bytes 8388640 | tf_op jit(solution)/shard_map/all_to_all | solution.py:299
  862.1 10.7 %fusion.22 = f32[2,128,16,8,128,1]{4,1,0,5,3,2:T(8,128)} fusion(f32[1,128,2,128]{1,3,2,0:T(8,128)S(1)} %get-tuple-element.118, f32[1,128,2,128]{1,3,2,0:T(8,128)S(1)} %get-tuple-element.115, bf16[16,16,2,8,8,128]{5,4,3,2,1,0:T(8,128)(2,1)} %all-to-all-done.3), kind=kOutput, calls=%fused_computation.35 | convolution fusion | flops 6442582016 | bytes 25427968 | tf_op jit(solution)/shard_map/prxyz,rysk->psxkz/dot_general | solution.py:66
  872.8 13.4 %fusion.21 = bf16[16,2,8,128,128]{3,4,2,0,1:T(8,128)(2,1)} fusion(f32[2,128,16,8,128,1]{4,1,0,5,3,2:T(8,128)} %fusion.22, f32[1,128,2,128]{1,3,2,0:T(8,128)S(1)} %get-tuple-element.118, f32[1,128,2,128]{1,3,2,0:T(8,128)S(1)} %get-tuple-element.115), kind=kOutput, calls=%fused_computation.34 | convolution fusion | flops 6446776320 | bytes 25427968 | tf_op jit(solution)/shard_map/prxyz,rzsk->psxyk/dot_general | solution.py:66
  886.2 21.1 %copy.539 = bf16[16,2,8,128,128]{4,1,0,3,2:T(2,128)(2,1)} copy(bf16[16,2,8,128,128]{3,4,2,0,1:T(8,128)(2,1)} %fusion.21) | data formatting | bytes 16777216 | tf_op jit(solution)/shard_map/convert_element_type | solution.py:305
  919.3 15.5 %pad_maximum_fusion = (bf16[64,8,128,128]{3,0,2,1:T(8,128)(2,1)S(1)}, bf16[8,128,64,128]{3,2,1,0:T(8,128)(2,1)}) fusion(bf16[32,8,128,128]{3,0,2,1:T(8,128)(2,1)} %bitcast.423, bf16[32,8,128,128]{3,0,2,1:T(8,128)(2,1)} %bitcast.420), kind=kLoop, calls=%fused_computation.2 | loop fusion | flops 33554432 | bytes 50331648 | tf_op jit(solution)/shard_map/concatenate | solution.py:306
  934.8 36.0 %copy.571 = bf16[64,8,128,128]{3,2,1,0:T(8,128)(2,1)} copy(bf16[64,8,128,128]{3,0,2,1:T(8,128)(2,1)S(1)} %get-tuple-element.44) | data formatting | bytes 33554432
  970.8 14.2 %collective-permute-done.2.refs_0_.refs_1_.refs_2_ = bf16[1,128,64,128]{3,2,1,0:T(8,128)(2,1)S(1)} collective-permute-done((bf16[1,128,64,128]{3,2,1,0:T(8,128)(2,1)}, bf16[1,128,64,128]{3,2,1,0:T(8,128)(2,1)S(1)}, u32[]{:S(2)}, u32[]{:S(2)}) %collective-permute-start.2) | collective-permute-done | bytes 2097184 | tf_op jit(solution)/shard_map/ppermute | solution.py:24
  985.0 39.6 %shard_map.86 = (f32[32,64,64]{2,1,0:T(8,128)S(1)}, f32[32,11,64]{2,1,0:T(8,128)S(1)}, f32[32,7,64]{2,1,0:T(8,128)S(1)}, f32[32,1,64]{2,1,0:T(1,128)S(1)}) custom-call(s32[32]{0:T(128)S(1)} %copy-done.2, bf16[1,128,64,128]{3,2,1,0:T(8,128)(2,1)S(1)} %collective-permute-done.2.refs_0_.refs_1_.refs_2_, ...), custom_call_target="tpu_custom_call" | custom-call | tf_op jit(solution)/shard_map/pallas_call | solution.py:241
  (248 shorter events, 71.6 us)
Async XLA Ops:
  1.4 2.2 copy-start.14
  3.1 0.6 copy-start.16
  3.1 0.6 copy-start.18
  3.1 0.6 copy-start.20
  4.6 1.9 copy-start.3
  5.9 7.2 collective-permute-start.1
  6.0 13.7 %collective-permute-start = (bf16[79,32,16]{0,2,1:T(8,128)(2,1)S(1)}, bf16[79,32,16]{0,2,1:T(8,128)(2,1)S(1)}, u32[]{:S(2)}, u32[]{:S(2)}) collective-permute-start(bf16[79,32,16]{0,2,1:T(8,128)(2,1)S(1)} %bitcast.463), channel_id=1, source_target_pairs={{15,0},{0,1},{1,2},{2,3},{3,4},{4,5},{5,6},{6,7},{7,8},{8,9},{9,10... | collective-permute-start | bytes 242696 | tf_op jit(solution)/shard_map/ppermute | solution.py:24
  16.4 12.5 %copy-start.6 = (f32[1,32,16]{2,1,0:T(8,128)}, f32[1,32,16]{2,1,0:T(8,128)S(1)}, u32[]{:S(2)}) copy-start(f32[1,32,16]{2,1,0:T(8,128)S(1)} %get-tuple-element.74) | copy-start | bytes 6148
  59.4 5.8 copy-start
  108.6 191.0 %all-to-all-start = ((bf16[16,16,2,8,8,128]{5,4,3,2,1,0:T(8,128)(2,1)}), bf16[16,16,2,8,8,128]{5,4,3,2,1,0:T(8,128)(2,1)}, u32[]{:S(2)}, u32[]{:S(2)}) async-start(bf16[16,16,2,8,8,128]{5,4,3,2,1,0:T(8,128)(2,1)} %bitcast.429), calls=%async_computation | async-start | bytes 16777216 | tf_op jit(solution)/shard_map/all_to_all | solution.py:290
  299.6 6.3 copy-start.5
  299.6 187.4 %all-to-all-start.2 = ((bf16[16,16,2,8,8,128]{5,4,3,2,1,0:T(8,128)(2,1)}), bf16[16,16,2,8,8,128]{5,4,3,2,1,0:T(8,128)(2,1)}, u32[]{:S(2)}, u32[]{:S(2)}) async-start(bf16[16,16,2,8,8,128]{5,4,3,2,1,0:T(8,128)(2,1)} %bitcast.426), calls=%async_computation.2 | async-start | bytes 16777216 | tf_op jit(solution)/shard_map/all_to_all | solution.py:290
  487.0 187.6 %all-to-all-start.1 = ((bf16[16,16,2,8,8,128]{5,4,3,2,1,0:T(8,128)(2,1)}), bf16[16,16,2,8,8,128]{5,4,3,2,1,0:T(8,128)(2,1)}, u32[]{:S(2)}, u32[]{:S(2)}) async-start(bf16[16,16,2,8,8,128]{5,4,3,2,1,0:T(8,128)(2,1)} %bitcast.427), calls=%async_computation.1 | async-start | bytes 16777216 | tf_op jit(solution)/shard_map/all_to_all | solution.py:299
  674.6 187.5 %all-to-all-start.3 = ((bf16[16,16,2,8,8,128]{5,4,3,2,1,0:T(8,128)(2,1)}), bf16[16,16,2,8,8,128]{5,4,3,2,1,0:T(8,128)(2,1)}, u32[]{:S(2)}, u32[]{:S(2)}) async-start(bf16[16,16,2,8,8,128]{5,4,3,2,1,0:T(8,128)(2,1)} %bitcast.428), calls=%async_computation.3 | async-start | bytes 16777216 | tf_op jit(solution)/shard_map/all_to_all | solution.py:299
  907.3 3.9 copy-start.21
  907.3 4.0 copy-start.19
  907.3 4.1 copy-start.17
  907.3 4.2 copy-start.13
  907.3 4.3 copy-start.15
  911.2 73.8 %collective-permute-start.3 = (bf16[2,128,64,128]{3,2,1,0:T(8,128)(2,1)}, bf16[2,128,64,128]{3,2,1,0:T(8,128)(2,1)}, u32[]{:S(2)}, u32[]{:S(2)}) collective-permute-start(bf16[2,128,64,128]{3,2,1,0:T(8,128)(2,1)} %fusion.47), channel_id=1, source_target_pairs={{1,0},{2,1},{3,2},{4,3},{5,4},{6,5},{7,6},{8,7},{9,8},{10,9},{11,1... | collective-permute-start | bytes 12582920 | tf_op jit(solution)/shard_map/ppermute | solution.py:24
  911.8 4.7 copy-start.7
  911.8 4.6 copy-start.8
  911.9 4.2 copy-start.9
  912.0 4.2 copy-start.10
  912.1 4.1 copy-start.11
  912.1 4.0 copy-start.12
  912.1 4.9 copy-start.4
  915.3 69.6 %collective-permute-start.2 = (bf16[1,128,64,128]{3,2,1,0:T(8,128)(2,1)}, bf16[1,128,64,128]{3,2,1,0:T(8,128)(2,1)S(1)}, u32[]{:S(2)}, u32[]{:S(2)}) collective-permute-start(bf16[1,128,64,128]{3,2,1,0:T(8,128)(2,1)} %fusion.49), channel_id=1, source_target_pairs={{15,0},{0,1},{1,2},{2,3},{3,4},{4,5},{5,6},{6,7},{7,8},{8,9},{9,10... | collective-permute-start | bytes 6291464 | tf_op jit(solution)/shard_map/ppermute | solution.py:24
  934.8 50.2 %copy-start.2 = (s32[32]{0:T(128)S(1)}, s32[32]{0:T(128)}, u32[]{:S(2)}) copy-start(s32[32]{0:T(128)} %bricks_ref.1) | copy-start | bytes 388
  1024.6 1.0 copy-start.1
